TPU v7x, 512 devices: a whole 4x8x8 slice. The times are simulated.
512 devices in a mesh: dp: 64 (over z_hi, y, core), tensor: 8 (over x, z_lo).
Axes of the slice: x: 4, y: 8, z: 8 (z_hi: 4, z_lo: 2; z = z_hi * 2 + z_lo), core: 2. Of those that a mesh axis runs over, the one named last changes fastest.
Arguments:
- teacher: bfloat16 [16384, 3072], P('dp', 'tensor'), may hold values from -6 to 6
- projector: bfloat16 [3072, 2048], P('tensor', 'dp'), may hold values from -0.109375 to 0.109375
- residual: bfloat16 [16384, 2048], P(('dp', 'tensor')), may hold values from -6 to 6
- gate_pre: bfloat16 [16384, 8192], P('dp', 'tensor'), may hold values from -6 to 6
- up_pre: bfloat16 [16384, 8192], P('dp', 'tensor'), may hold values from -6 to 6
- down_weight: bfloat16 [8192, 2048], P('tensor', 'dp'), may hold values from -0.0625 to 0.0625
Outputs:
- projector_grad: float32 [3072, 2048], P('tensor', 'dp')
- grad_residual: bfloat16 [16384, 2048], P(('dp', 'tensor'))
- grad_gate: bfloat16 [16384, 8192], P('dp', 'tensor')
- grad_up: bfloat16 [16384, 8192], P('dp', 'tensor')
All inputs are finite; a program needn't handle non-finite values.
Results may differ from a plain program's by a relative error of at most 0.015.
Values may be sent and summed in bfloat16 or wider, within the bound.
A program may use at most 64 MiB of HBM per device.

v0:
```python
import math
import jax
import jax.numpy as jnp
from jax import lax
from jax.sharding import PartitionSpec as P


def per_device(teacher, projector, residual, gate_pre, up_pre, down_weight):
    group_rows = teacher.shape[0]
    ways = lax.axis_size("tensor")
    share = group_rows // ways
    token_total = group_rows * lax.axis_size("dp")
    gate = gate_pre.astype(jnp.float32)
    upper = up_pre.astype(jnp.float32)
    sig = jax.nn.sigmoid(gate)
    hidden = (gate * sig * upper).astype(jnp.bfloat16)
    projected = jnp.dot(
        teacher,
        lax.all_gather(projector, "dp", axis=1, tiled=True),
        preferred_element_type=jnp.float32,
    )
    down_whole = lax.all_gather(down_weight, "dp", axis=1, tiled=True)
    mlp_term = jnp.dot(hidden, down_whole, preferred_element_type=jnp.float32)
    parts = mlp_term - projected
    stacked = parts.astype(jnp.bfloat16).reshape(ways, share, parts.shape[1])
    received = lax.all_to_all(stacked, "tensor", split_axis=0, concat_axis=0, tiled=True)
    summed = jnp.sum(received.astype(jnp.float32), axis=0)
    grad_own = (residual.astype(jnp.float32) + summed).astype(jnp.bfloat16)
    grad_rows = lax.all_gather(grad_own, "tensor", axis=0, tiled=True)
    contract_cols = (((1,), (1,)), ((), ()))
    hidden_grad = lax.dot_general(
        grad_rows, down_whole, contract_cols, preferred_element_type=jnp.float32
    )
    grad_up = (hidden_grad * gate * sig).astype(jnp.bfloat16)
    grad_gate = (hidden_grad * upper * sig * (1.0 + gate * (1.0 - sig))).astype(jnp.bfloat16)
    local_grad = lax.dot_general(
        teacher, grad_rows, (((0,), (0,)), ((), ())), preferred_element_type=jnp.float32
    )
    projector_grad = lax.psum_scatter(
        local_grad, "dp", scatter_dimension=1, tiled=True
    ) / math.sqrt(token_total)
    return (projector_grad, grad_own, grad_gate, grad_up)


def solution(mesh):
    in_specs = (
        P("dp", "tensor"),
        P("tensor", "dp"),
        P(("dp", "tensor"), None),
        P("dp", "tensor"),
        P("dp", "tensor"),
        P("tensor", "dp"),
    )
    out_specs = (P("tensor", "dp"), P(("dp", "tensor"), None), P("dp", "tensor"), P("dp", "tensor"))
    return jax.shard_map(
        per_device, mesh=mesh, in_specs=in_specs, out_specs=out_specs, check_vma=False
    )
```

profile of v0, /device:TPU:2, one launch (start us, length us, event | category | flops | bytes accessed | tf_op | source)
XLA Modules:
  0.0 417.5 jit_solution(8088165536229022003)
XLA Ops:
  7.2 0.0 copy-start
  7.2 0.0 all-gather.4.cloned.1.call-start
  7.2 0.7 all-gather.4.cloned.1.call-update
  7.9 0.0 all-gather.6.cloned.1.call-start
  8.0 0.7 all-gather.6.cloned.1.call-update
  8.7 0.0 all-gather.8.cloned.1.call-start
  8.7 95.7 %all-gather.4.cloned.1.call-done = bf16[1024,2048]{0,1:T(8,128)(2,1)} async-done(((bf16[1024,32]{0,1:T(8,128)(2,1)}), bf16[1024,2048]{0,1:T(8,128)(2,1)}) %all-gather.4.cloned.1.call-update) | async-done | bytes 4194320 | tf_op jit(solution)/shard_map/all_gather | solution.py:22
  104.4 3.9 fusion.11
  108.3 79.0 %all-gather.6.cloned.1.call-done = bf16[384,2048]{0,1:T(8,128)(2,1)} async-done(((bf16[384,32]{0,1:T(8,128)(2,1)}), bf16[384,2048]{0,1:T(8,128)(2,1)}) %all-gather.6.cloned.1.call-update) | async-done | bytes 1572880 | tf_op jit(solution)/shard_map/all_gather | solution.py:19
  187.4 0.0 copy-done
  187.4 2.1 fusion
  189.5 0.0 copy-start.2
  189.5 19.2 %all_to_all.5 = bf16[8,32,2048]{2,1,0:T(8,128)(2,1)S(1)} all-to-all(bf16[8,32,2048]{2,1,0:T(8,128)(2,1)S(1)} %bitcast.10), channel_id=1, replica_groups=mesh['dp'=64,'tensor'=8] {'tensor'}, dimensions={0} | all-to-all | bytes 2097152 | tf_op jit(solution)/shard_map/all_to_all | solution.py:26
  208.7 0.1 convert_reduce_fusion
  208.9 0.0 copy-done.2
  208.9 0.7 add_convert_fusion
  209.6 0.0 all-gather.8.cloned.1.call-update
  209.6 0.0 reduce-scatter.2.cloned.1.call-start
  209.6 40.8 %all-gather.8.cloned.1.call-done = bf16[256,2048]{1,0:T(8,128)(2,1)} async-done(((bf16[32,2048]{1,0:T(8,128)(2,1)}), bf16[256,2048]{1,0:T(8,128)(2,1)}) %all-gather.8.cloned.1.call-update) | async-done | bytes 1048592 | tf_op jit(solution)/shard_map/all_gather | solution.py:29
  250.4 3.7 convolution_bitcast_fusion
  254.1 0.0 copy-start.1
  254.1 0.0 copy-start.3
  254.1 0.0 copy-start.4
  254.1 0.0 reduce-scatter.2.cloned.1.call-update
  254.1 1.2 copy-done.1
  255.3 0.1 copy-done.3
  255.4 0.2 copy-done.4
  255.6 4.7 %fusion.10 = (bf16[256,1024]{1,0:T(8,128)(2,1)}, bf16[256,1024]{1,0:T(8,128)(2,1)}) fusion(bf16[256,1024]{1,0:T(8,128)(2,1)S(1)} %copy-done.4, bf16[256,1024]{1,0:T(8,128)(2,1)S(1)} %copy-done.3, bf16[256,2048]{1,0:T(8,128)(2,1)S(1)} %copy-done.1, bf16[1024,2048]{0,1:T(8,128)(2,1)} %all-gather.4.cloned.1.call-done), kind=kOutput, calls=%fused_computation.19 | convolution fusion | flops 1077673984 | bytes 7340032 | tf_op jit(solution)/shard_map/dot_general | solution.py:31
  260.3 149.3 %reduce-scatter.2.cloned.1.call-done = f32[384,32]{0,1:T(8,128)} async-done(((f32[384,2048]{0,1:T(8,128)}), f32[384,32]{0,1:T(8,128)}) %reduce-scatter.2.cloned.1.call-update) | async-done | bytes 49168 | tf_op jit(solution)/shard_map/reduce_scatter | solution.py:39
  409.6 1.4 broadcast_multiply_fusion
Async XLA Ops:
  7.2 180.2 %copy-start = (bf16[256,384]{1,0:T(8,128)(2,1)S(1)}, bf16[256,384]{1,0:T(8,128)(2,1)}, u32[]{:S(2)}) copy-start(bf16[256,384]{1,0:T(8,128)(2,1)} %param.6) | copy-start | bytes 589828
  7.2 97.2 %all-gather.4.cloned.1.call-start = ((), (), s32[]{:S(2)}) async-start(), calls=%async_computation.2 | async-start | bytes 4259840 | tf_op jit(solution)/shard_map/all_gather | solution.py:22
  7.9 179.4 %all-gather.6.cloned.1.call-start = ((), (), s32[]{:S(2)}) async-start(), calls=%async_computation.3 | async-start | bytes 1597440 | tf_op jit(solution)/shard_map/all_gather | solution.py:19
  8.7 241.8 %all-gather.8.cloned.1.call-start = ((), (), s32[]{:S(2)}) async-start(), calls=%async_computation.4 | async-start | bytes 1179648 | tf_op jit(solution)/shard_map/all_gather | solution.py:29
  189.5 19.4 %copy-start.2 = (bf16[32,2048]{1,0:T(8,128)(2,1)S(1)}, bf16[32,2048]{1,0:T(8,128)(2,1)}, u32[]{:S(2)}) copy-start(bf16[32,2048]{1,0:T(8,128)(2,1)} %param.8) | copy-start | bytes 393220
  209.6 200.0 %reduce-scatter.2.cloned.1.call-start = ((), (), s32[]{:S(2)}) async-start(), calls=%async_computation.5 | async-start | bytes 3194880 | tf_op jit(solution)/shard_map/reduce_scatter | solution.py:39
  254.1 1.2 copy-start.1
  254.1 1.4 copy-start.3
  254.1 1.5 copy-start.4
Sparse Core Ops, SparseCore 0:
  11.4 92.9 all-gather.3
  107.7 79.6 all-gather.5
  209.7 40.6 all-gather.7
  255.0 154.5 reduce-scatter.1
where the time goes:
time: 418 us
  waiting for transfers between devices  366 us (88%)
  blocking collectives  19.2 us (5%)
  matrix products  14.4 us (3%)
  between operations  13.8 us (3%)
    reduce_scatter x1, waiting for transfers between devices, per_device(): lax.psum_scatter(local_grad, 'dp', scatter_dimension=1, tiled=True)  149 us
    all_gather x1, waiting for transfers between devices, per_device(): down_whole = lax.all_gather(down_weight, 'dp', axis=1, tiled=True)  95.7 us
    all_gather x1, waiting for transfers between devices, per_device(): lax.all_gather(projector, 'dp', axis=1, tiled=True)  79 us
    all_gather x1, waiting for transfers between devices, per_device(): grad_rows = lax.all_gather(grad_own, 'tensor', axis=0, tiled=True)  40.8 us
    all_to_all x1, blocking collectives, per_device(): lax.all_to_all(stacked, 'tensor', split_axis=0, concat_axis=0, tiled=True)  19.2 us
  transfers between devices with their start and end apart: 4, of which 4 were waited for; matrix products, arithmetic and copies ran while one was open for 2% of the time, Pallas kernels for 0%

commit v1 on v0

--- a/solution.py
+++ b/solution.py
@@ -26,7 +26,9 @@
     received = lax.all_to_all(stacked, "tensor", split_axis=0, concat_axis=0, tiled=True)
     summed = jnp.sum(received.astype(jnp.float32), axis=0)
     grad_own = (residual.astype(jnp.float32) + summed).astype(jnp.bfloat16)
-    grad_rows = lax.all_gather(grad_own, "tensor", axis=0, tiled=True)
+    grad_rows = jnp.concatenate(
+        lax.all_to_all(jnp.stack([grad_own] * lax.axis_size("tensor")), "tensor", 0, 0), axis=0
+    )
     contract_cols = (((1,), (1,)), ((), ()))
     hidden_grad = lax.dot_general(
         grad_rows, down_whole, contract_cols, preferred_element_type=jnp.float32

time: 418 us -> 389 us (0.931)
  the two profiles are of different devices: /device:TPU:2 before, /device:TPU:4 now
where the time goes in v1:
time: 389 us; the launch traced here: 388 us
  waiting for transfers between devices  322 us (83%)
  blocking collectives  36.4 us (9%)
  between operations  13.8 us (4%)
  matrix products  13.2 us (3%)
    reduce_scatter x1, waiting for transfers between devices, per_device(): lax.psum_scatter(local_grad, 'dp', scatter_dimension=1, tiled=True)  146 us
    all_gather x1, waiting for transfers between devices, per_device(): down_whole = lax.all_gather(down_weight, 'dp', axis=1, tiled=True)  95.7 us
    all_gather x1, waiting for transfers between devices, per_device(): lax.all_gather(projector, 'dp', axis=1, tiled=True)  79 us
    all_to_all x1, blocking collectives, per_device(): lax.all_to_all(stacked, 'tensor', split_axis=0, concat_axis=0, tiled=True)  18.6 us
    all_to_all x1, blocking collectives, per_device(): lax.all_to_all(jnp.stack([grad_own] * lax.axis_size('tensor')), 'tensor',...  17.8 us
  transfers between devices with their start and end apart: 3, of which 3 were waited for; matrix products, arithmetic and copies ran while one was open for 2% of the time, Pallas kernels for 0%

profile of v1, /device:TPU:4, one launch (start us, length us, event | category | flops | bytes accessed | tf_op | source)
XLA Modules:
  0.0 388.2 jit_solution(17288825465285491321)
XLA Ops:
  7.2 0.0 copy-start
  7.2 0.0 all-gather.3.cloned.1.call-start
  7.2 0.7 all-gather.3.cloned.1.call-update
  7.9 0.0 all-gather.5.cloned.1.call-start
  8.0 0.7 all-gather.5.cloned.1.call-update
  8.7 0.0 reduce-scatter.2.cloned.1.call-start
  8.7 95.7 %all-gather.3.cloned.1.call-done = bf16[1024,2048]{0,1:T(8,128)(2,1)} async-done(((bf16[1024,32]{0,1:T(8,128)(2,1)}), bf16[1024,2048]{0,1:T(8,128)(2,1)}) %all-gather.3.cloned.1.call-update) | async-done | bytes 4194320 | tf_op jit(solution)/shard_map/all_gather | solution.py:22
  104.4 3.9 %fusion.11 = f32[256,2048]{1,0:T(8,128)S(1)} fusion(bf16[1024,2048]{0,1:T(8,128)(2,1)} %all-gather.3.cloned.1.call-done, bf16[256,1024]{1,0:T(8,128)(2,1)} %param.10, bf16[256,1024]{1,0:T(8,128)(2,1)} %param.9), kind=kOutput, calls=%fused_computation.20 | convolution fusion | flops 1075838976 | bytes 7340032 | tf_op jit(solution)/shard_map/dot_general | solution.py:23
  108.3 79.0 %all-gather.5.cloned.1.call-done = bf16[384,2048]{0,1:T(8,128)(2,1)} async-done(((bf16[384,32]{0,1:T(8,128)(2,1)}), bf16[384,2048]{0,1:T(8,128)(2,1)}) %all-gather.5.cloned.1.call-update) | async-done | bytes 1572880 | tf_op jit(solution)/shard_map/all_gather | solution.py:19
  187.3 0.0 copy-done
  187.3 2.1 fusion
  189.5 0.0 copy-start.2
  189.5 18.6 %all_to_all.10 = bf16[8,32,2048]{2,1,0:T(8,128)(2,1)S(1)} all-to-all(bf16[8,32,2048]{2,1,0:T(8,128)(2,1)S(1)} %bitcast.13), channel_id=1, replica_groups=mesh['dp'=64,'tensor'=8] {'tensor'}, dimensions={0} | all-to-all | bytes 2097152 | tf_op jit(solution)/shard_map/all_to_all | solution.py:26
  208.1 0.1 convert_reduce_fusion
  208.2 0.0 copy-done.2
  208.3 0.0 copy-start.1
  208.3 0.1 stack.2
  208.4 17.8 %all_to_all.11 = bf16[8,32,2048]{2,1,0:T(8,128)(2,1)S(1)} all-to-all(bf16[8,32,2048]{2,1,0:T(8,128)(2,1)S(1)} %stack.2), channel_id=1, replica_groups=mesh['dp'=64,'tensor'=8] {'tensor'}, dimensions={0} | all-to-all | bytes 2097152 | tf_op jit(solution)/shard_map/all_to_all | solution.py:30
  226.2 2.4 convolution_bitcast_fusion
  228.6 0.0 copy-done.1
  228.6 0.0 copy-start.3
  228.6 0.0 copy-start.4
  228.6 0.0 reduce-scatter.2.cloned.1.call-update
  228.6 1.0 copy-done.3
  229.7 0.2 copy-done.4
  229.8 4.7 %fusion.10 = (bf16[256,1024]{1,0:T(8,128)(2,1)}, bf16[256,1024]{1,0:T(8,128)(2,1)}) fusion(bf16[256,1024]{1,0:T(8,128)(2,1)S(1)} %copy-done.4, bf16[256,1024]{1,0:T(8,128)(2,1)S(1)} %copy-done.3, bf16[256,2048]{1,0:T(8,128)(2,1)S(1)} %bitcast.12, bf16[1024,2048]{0,1:T(8,128)(2,1)} %all-gather.3.cloned.1.call-done), kind=kOutput, calls=%fused_computation.19 | convolution fusion | flops 1077673984 | bytes 7340032 | tf_op jit(solution)/shard_map/dot_general | solution.py:33
  234.5 145.8 %reduce-scatter.2.cloned.1.call-done = f32[384,32]{0,1:T(8,128)} async-done(((f32[384,2048]{0,1:T(8,128)}), f32[384,32]{0,1:T(8,128)}) %reduce-scatter.2.cloned.1.call-update) | async-done | bytes 49168 | tf_op jit(solution)/shard_map/reduce_scatter | solution.py:41
  380.3 1.4 broadcast_multiply_fusion
  (1 shorter events, 0.0 us)
Async XLA Ops:
  7.2 180.2 %copy-start = (bf16[256,384]{1,0:T(8,128)(2,1)S(1)}, bf16[256,384]{1,0:T(8,128)(2,1)}, u32[]{:S(2)}) copy-start(bf16[256,384]{1,0:T(8,128)(2,1)} %param.6) | copy-start | bytes 589828
  7.2 97.2 %all-gather.3.cloned.1.call-start = ((), (), s32[]{:S(2)}) async-start(), calls=%async_computation.3 | async-start | bytes 4259840 | tf_op jit(solution)/shard_map/all_gather | solution.py:22
  7.9 179.4 %all-gather.5.cloned.1.call-start = ((), (), s32[]{:S(2)}) async-start(), calls=%async_computation.4 | async-start | bytes 1597440 | tf_op jit(solution)/shard_map/all_gather | solution.py:19
  8.7 371.6 %reduce-scatter.2.cloned.1.call-start = ((), (), s32[]{:S(2)}) async-start(), calls=%async_computation.5 | async-start | bytes 3194880 | tf_op jit(solution)/shard_map/reduce_scatter | solution.py:41
  189.5 18.7 %copy-start.2 = (bf16[32,2048]{1,0:T(8,128)(2,1)S(1)}, bf16[32,2048]{1,0:T(8,128)(2,1)}, u32[]{:S(2)}) copy-start(bf16[32,2048]{1,0:T(8,128)(2,1)} %param.8) | copy-start | bytes 393220
  208.3 20.4 %copy-start.1 = (bf16[32,2048]{1,0:T(8,128)(2,1)}, bf16[32,2048]{1,0:T(8,128)(2,1)S(1)}, u32[]{:S(2)}) copy-start(bf16[32,2048]{1,0:T(8,128)(2,1)S(1)} %add_convert_fusion) | copy-start | bytes 393220
  228.6 1.0 copy-start.3
  228.6 1.2 copy-start.4
Sparse Core Ops, SparseCore 0:
  11.4 92.9 all-gather.2
  107.7 79.6 all-gather.4
  228.8 151.4 reduce-scatter.1
